TPU v7x, 32 devices: a whole 2x2x4 slice. The times are simulated.
32 devices in a mesh: valve: 4 (over y, core), bulk: 8 (over z, x).
Axes of the slice: x: 2, y: 2, z: 4, core: 2. Of those that a mesh axis runs over, the one named last changes fastest.
Arguments:
- solution: float32 [5, 64, 32768], P(None, None, ('valve', 'bulk')), may hold values from -6 to 6
- velocity: float32 [3, 32768], P(None, ('valve', 'bulk')), may hold values from -1 to 1
- inv_jacobian: float32 [64, 32768], P(None, ('valve', 'bulk')), may hold values from 0.5 to 3
- face_speed: float32 [96, 32768], P(None, ('valve', 'bulk')), may hold values from -6 to 6
- face_link: int32 [6, 32768], P(None, ('valve', 'bulk')), may hold values from 0 to 6271, as said below
- donor_elem: int32 [262144], P(('valve', 'bulk')), may hold values from 0 to 1023
- ref_coords: float32 [3, 262144], P(None, ('valve', 'bulk')), may hold values from -1 to 1
- owner_list: int32 [262144, 1], P(('valve', 'bulk')), may hold values from 0 to 7; in each aligned block of 8192 rows (0 to 8191, 8192 to 16383, ...) at most 2048 rows name the same one
Outputs:
- section_rate: float32 [5, 64, 32768], P(None, None, ('valve', 'bulk'))
- fringe_values: float32 [5, 524288], P(None, ('valve', 'bulk'))
Inputs may be any that keep to these rules, and one draw needn't show every extreme that they name: `face_link`: on each device, the values 6 * 1024 to 6271 appear exactly once each; every other face slot links to another slot of the same device that links back to it. `owner_list`: among the receptors of one device no owner is named more than 2048 times; in every draw some device names some owner exactly 2048 times.
All inputs are finite; a program needn't handle non-finite values.
Results may differ from a plain program's by a relative error of at most 0.0003.
Values sent between devices are 32-bit elements; how exact they have to be, the bound alone decides.
A program may use at most 192 MiB of HBM per device.

v0:
```python
import jax
import jax.numpy as jnp
import numpy as np
from jax import lax
from jax.sharding import PartitionSpec as P

gauss_nodes = (-0.8611363115940526, -0.3399810435848563, 0.3399810435848563, 0.8611363115940526)
quad_weights = (0.3478548451374538, 0.6521451548625461, 0.6521451548625461, 0.3478548451374538)
section_step = 0.2


def padded(shard, sides, width):
    for axis, dim in sides:
        size, length = (lax.axis_size(axis), shard.shape[dim])
        up = [(i, (i + 1) % size) for i in range(size)]
        down = [(j, i) for i, j in up]
        last = lax.slice_in_dim(shard, length - width, length, axis=dim)
        initial = lax.slice_in_dim(shard, 0, width, axis=dim)
        before = lax.ppermute(last, axis, up)
        after = lax.ppermute(initial, axis, down)
        shard = jnp.concatenate([before, shard, after], axis=dim)
    return shard


def lagrange_at(x):
    values = []
    for j in range(4):
        factor = 1.0
        for m in range(4):
            if m != j:
                factor = factor * (x - gauss_nodes[m]) / (gauss_nodes[j] - gauss_nodes[m])
        values.append(factor)
    return values


def tables():
    slopes = np.zeros((4, 4))
    for i in range(4):
        for j in range(4):
            summed = 0.0
            for m in range(4):
                if m != j:
                    product = 1.0 / (gauss_nodes[j] - gauss_nodes[m])
                    for n in range(4):
                        if n != j and n != m:
                            product = (
                                product
                                * (gauss_nodes[i] - gauss_nodes[n])
                                / (gauss_nodes[j] - gauss_nodes[n])
                            )
                    summed = summed + product
            slopes[i, j] = summed
    end_values = [lagrange_at(-1.0), lagrange_at(1.0)]
    extrapolate = np.zeros((96, 64))
    lifting = np.zeros((64, 96))
    derivative = np.zeros((3, 64, 64))
    for p in range(64):
        point_idx = (p // 16, p // 4 % 4, p % 4)
        for f in range(6):
            normal_dir = f // 2
            across = [t for t in range(3) if t != normal_dir]
            q = point_idx[across[0]] * 4 + point_idx[across[1]]
            flux_row = q * 6 + f
            extrapolate[flux_row, p] = end_values[f % 2][point_idx[normal_dir]]
            lifting[p, flux_row] = (
                end_values[f % 2][point_idx[normal_dir]] / quad_weights[point_idx[normal_dir]]
            )
        for s in range(64):
            other_idx = (s // 16, s // 4 % 4, s % 4)
            for normal_dir in range(3):
                if all((point_idx[t] == other_idx[t] for t in range(3) if t != normal_dir)):
                    derivative[normal_dir, p, s] = slopes[
                        point_idx[normal_dir], other_idx[normal_dir]
                    ]
    return (
        jnp.asarray(extrapolate, dtype=jnp.float32),
        jnp.asarray(derivative, dtype=jnp.float32),
        jnp.asarray(lifting, dtype=jnp.float32),
    )


def face_rows(solution, face_speed, extrapolate):
    nvars = solution.shape[0]
    elems = solution.shape[2]
    ext_faces = extrapolate.reshape(16, 6, 64)
    values = jnp.einsum("qfp,vpe->feqv", ext_faces, solution, precision=lax.Precision.HIGHEST)
    values = values.reshape(6 * elems, 16, nvars)
    speeds = jnp.transpose(face_speed.reshape(16, 6, elems), (1, 2, 0)).reshape(6 * elems, 16)
    return (values, speeds)


def rim_rows(table_own, links, faces_total, rim_count):
    slots = jnp.where(links >= faces_total, links - faces_total, 2 * rim_count)
    senders = (
        jnp.zeros((2 * rim_count,), jnp.int32)
        .at[slots]
        .set(jnp.arange(faces_total, dtype=jnp.int32), mode="drop")
    )
    return jnp.take(table_own, senders, axis=0)


def surface_term(values, speeds, table_own, links, received, lifting, elems):
    nvars = values.shape[2]
    full_table = jnp.concatenate([table_own, received], axis=0)
    outer = jnp.take(full_table, links, axis=0)
    outer_vals = outer[:, : 16 * nvars].reshape(6 * elems, 16, nvars)
    outer_speed = outer[:, 16 * nvars :][:, :, None]
    own_speed = speeds[:, :, None]
    normal = 0.5 * (own_speed - outer_speed)
    common = 0.5 * normal * (values + outer_vals) + 0.5 * jnp.abs(normal) * (values - outer_vals)
    jump_term = (common - own_speed * values).reshape(6, elems, 16, nvars)
    lift_faces = lifting.reshape(64, 16, 6)
    return jnp.einsum("pqf,feqv->vpe", lift_faces, jump_term, precision=lax.Precision.HIGHEST)


def volume_term(solution, velocity, derivative):
    slopes = jnp.einsum("dpq,vqe->dvpe", derivative, solution, precision=lax.Precision.HIGHEST)
    return jnp.sum(velocity[:, None, None, :] * slopes, axis=0)


def receptor_rows(advanced, donors, coords):
    nvars = advanced.shape[0]
    elems = advanced.shape[2]
    basis_x = jnp.stack(lagrange_at(coords[0]))
    basis_y = jnp.stack(lagrange_at(coords[1]))
    basis_z = jnp.stack(lagrange_at(coords[2]))
    weights = (
        basis_x[:, None, None, :] * basis_y[None, :, None, :] * basis_z[None, None, :, :]
    ).reshape(64, -1)
    element_rows = jnp.transpose(advanced, (2, 0, 1)).reshape(elems, nvars * 64)
    picked = jnp.take(element_rows, donors, axis=0).reshape(donors.shape[0], nvars, 64)
    return jnp.einsum("rvp,pr->rv", picked, weights, precision=lax.Precision.HIGHEST)


def owner_ranks(owners, buckets):
    onehot = (owners[:, None] == jnp.arange(buckets, dtype=jnp.int32)[None, :]).astype(jnp.int32)
    before = jnp.cumsum(onehot, axis=0) - onehot
    return jnp.sum(before * onehot, axis=1)


def on_device(
    solution, velocity, inv_jacobian, face_speed, face_link, donor_elem, ref_coords, owner_list
):
    extrapolate, derivative, lifting = tables()
    nvars = solution.shape[0]
    elems = solution.shape[2]
    rim_count = elems // 16
    faces_total = 6 * elems
    links = face_link.reshape(faces_total)
    values, speeds = face_rows(solution, face_speed, extrapolate)
    table_own = jnp.concatenate([values.reshape(faces_total, 16 * nvars), speeds], axis=1)
    outgoing = rim_rows(table_own, links, faces_total, rim_count)
    extended = padded(outgoing, (("valve", 0),), rim_count)
    received = jnp.concatenate([extended[:rim_count], extended[3 * rim_count :]], axis=0)
    surface = surface_term(values, speeds, table_own, links, received, lifting, elems)
    volume = volume_term(solution, velocity, derivative)
    section_rate = -inv_jacobian[None] * (volume + surface)
    advanced = solution + section_step * section_rate
    receptor_vals = receptor_rows(advanced, donor_elem, ref_coords)
    buckets = lax.axis_size("bulk")
    receptors = receptor_vals.shape[0]
    capacity = 2 * receptors // buckets
    owners = owner_list[:, 0]
    places = owners * capacity + owner_ranks(owners, buckets)
    outgoing_slots = jnp.zeros((buckets * capacity, nvars), jnp.float32)
    outgoing_slots = outgoing_slots.at[places].set(receptor_vals)
    fringe_rows = lax.all_to_all(outgoing_slots, "bulk", split_axis=0, concat_axis=0, tiled=True)
    return (section_rate, jnp.transpose(fringe_rows))


def solution(mesh):
    placed = (
        P(None, None, ("valve", "bulk")),
        P(None, ("valve", "bulk")),
        P(None, ("valve", "bulk")),
        P(None, ("valve", "bulk")),
        P(None, ("valve", "bulk")),
        P(("valve", "bulk")),
        P(None, ("valve", "bulk")),
        P(("valve", "bulk"), None),
    )
    return jax.shard_map(
        on_device,
        mesh=mesh,
        in_specs=placed,
        out_specs=(P(None, None, ("valve", "bulk")), P(None, ("valve", "bulk"))),
        check_vma=False,
    )
```

profile of v0, /device:TPU:0, one launch (start us, length us, event | category | flops | bytes accessed | tf_op | source)
XLA Modules:
  0.0 225.5 jit_solution(4261173435978200814)
XLA Ops:
  0.6 0.0 copy-start.15
  0.6 0.8 copy.56
  1.4 0.1 compare_select_fusion.1
  1.5 23.0 %scatter_custom_fusion = s32[128]{0:T(128)S(1)} fusion(s32[6144]{0:T(1024)S(1)} %bitcast.104, s32[6144]{0:T(1024)S(1)} %iota.11, s32[]{:T(128)} %constant.122.clone.1), kind=kCustom, calls=%fused_computation.86 | custom fusion | bytes 516 | tf_op jit(solution)/shard_map/scatter | solution.py:97
  24.5 1.8 reshape.160
  26.4 1.9 copy.32
  28.3 0.0 copy-done.15
  28.3 0.0 copy-start
  28.3 4.0 %convolution_bitcast_fusion = f32[6,1024,16,5]{1,2,3,0:T(8,128)S(1)} fusion(f32[16,6,64,1]{2,0,3,1:T(8,128)S(1)} %copy-done.15, f32[5,64,1024]{2,1,0:T(8,128)} %param.11), kind=kOutput, calls=%fused_computation.22 | convolution fusion | flops 377487360 | bytes 3301376 | tf_op jit(solution)/shard_map/qfp,vpe->feqv/dot_general | solution.py:86
  32.3 0.0 copy-start.2
  32.3 1.2 copy.33
  33.5 2.5 %copy.55 = f32[10,8,6,1024]{3,1,2,0:T(8,128)} copy(f32[10,8,6,1024]{3,2,1,0:T(8,128)S(1)} %bitcast.90) | data formatting | bytes 3932160
  36.0 3.4 %copy.34 = f32[6144,80]{1,0:T(8,128)} copy(f32[6144,80]{0,1:T(8,128)} %bitcast.92) | data formatting | bytes 3932160 | tf_op jit(solution)/shard_map/reshape;reshape | solution.py:151
  39.4 0.0 copy-start.11
  39.4 0.0 copy-start.12
  39.4 0.0 copy-start.9
  39.5 4.5 %pad_maximum_fusion.1 = f32[6144,96]{1,0:T(8,128)} fusion(f32[6144,16]{1,0:T(8,128)S(1)} %bitcast.83, f32[6144,80]{1,0:T(8,128)} %copy.34), kind=kLoop, calls=%fused_computation.11 | loop fusion | flops 589824 | bytes 4718592 | tf_op jit(solution)/shard_map/concatenate | solution.py:151
  43.9 2.6 %gather_fusion = f32[128,96]{1,0:T(8,128)S(1)} fusion(f32[6144,96]{1,0:T(8,128)} %pad_maximum_fusion.1, s32[1024]{0:T(1024)S(1)} %pad_clamp_fusion), kind=kCustom, calls=%fused_computation | custom fusion | bytes 98816 | tf_op jit(solution)/shard_map/jit(_take)/gather | solution.py:99
  46.5 0.1 broadcast_select_fusion.1
  46.6 0.6 fusion.32
  47.2 2.4 %collective-permute-start.1 = (f32[64,96]{1,0:T(8,128)}, f32[64,96]{1,0:T(8,128)}, u32[]{:S(2)}, u32[]{:S(2)}) collective-permute-start(f32[64,96]{1,0:T(8,128)} %get-tuple-element.17), channel_id=1, source_target_pairs={{8,0},{16,8},{24,16},{0,24},{9,1},{17,9},{25,17},{1,25},{10,2},{18... | collective-permute-start | bytes 73736 | tf_op jit(solution)/shard_map/ppermute | solution.py:20
  49.6 0.0 collective-permute-start
  49.7 0.6 fusion.29
  50.4 2.4 %reduce-window.6 = s32[8,64,128]{2,1,0:T(8,128)S(1)} reduce-window(s32[8,64,128]{2,1,0:T(8,128)S(1)} %fusion.28, s32[]{:T(128)} %constant.122.clone.1), window={size=1x1x128 pad=0_0x0_0x127_0}, to_apply=%region_2.3 | reduce-window | flops 8323072 | bytes 524292 | tf_op jit(solution)/shard_map/reduce-window
  52.8 0.0 copy-start.13
  52.8 0.3 slice_reduce_fusion
  53.1 0.2 reduce-window.9
  53.3 0.1 add_bitcast_fusion
  53.5 0.2 fusion.27
  53.7 0.7 compare_select_fusion
  54.4 0.8 multiply_multiply_fusion.11
  55.1 0.2 pad_maximum_fusion.2
  55.4 0.0 copy-start.7
  55.4 0.1 broadcast_multiply_fusion.2
  55.5 0.1 pad_maximum_fusion.4
  55.7 0.0 copy-start.10
  55.7 0.5 broadcast_multiply_fusion.1
  56.2 5.2 %multiply_reduce_fusion.1 = f32[64,5,1024]{2,0,1:T(8,128)} fusion(f32[3,64,64,1]{2,1,3,0:T(8,128)S(1)} %copy-done.13, f32[3,1024]{1,0:T(4,128)} %param.12, f32[5,64,1024]{2,1,0:T(8,128)S(1)} %copy-done.4), kind=kOutput, calls=%fused_computation.8 | convolution fusion | flops 756613120 | bytes 2682880 | tf_op jit(solution)/shard_map/dpq,vqe->dvpe/dot_general | solution.py:117
  61.4 0.0 copy-done.7
  61.4 1.0 copy.40
  62.4 0.7 neg.4
  63.1 1.7 mul.259
  64.8 0.0 collective-permute-done.1
  64.8 0.0 collective-permute-done
  64.9 3.8 %pad_maximum_fusion = f32[6272,96]{1,0:T(8,128)S(1)} fusion(f32[64,96]{1,0:T(8,128)} %collective-permute-done.1, f32[64,96]{1,0:T(8,128)} %collective-permute-done, f32[6144,16]{1,0:T(8,128)} %bitcast.84, f32[6144,80]{1,0:T(8,128)} %copy.34), kind=kLoop, calls=%fused_computation.9 | loop fusion | flops 1806336 | bytes 4816896 | tf_op jit(solution)/shard_map/concatenate | solution.py:104
  68.6 21.1 %gather_fusion.1 = f32[6144,96]{1,0:T(8,128)} fusion(f32[6272,96]{1,0:T(8,128)S(1)} %pad_maximum_fusion, s32[6144]{0:T(1024)S(1)} %broadcast_clamp_fusion), kind=kCustom, calls=%fused_computation.1 | custom fusion | bytes 4743168 | tf_op jit(solution)/shard_map/jit(_take)/gather | solution.py:105
  89.7 4.8 %broadcast_select_fusion = f32[6144,96]{1,0:T(8,128)S(1)} fusion(f32[6144,96]{1,0:T(8,128)} %gather_fusion.1, pred[6144]{0:T(1024)(128)(4,1)S(1)} %compare_and_fusion.1), kind=kLoop, calls=%fused_computation.24 | loop fusion | flops 589824 | bytes 4724736 | tf_op jit(solution)/shard_map/jit(_take)/select_n | solution.py:105
  94.5 0.0 copy-done.1
  94.5 3.5 %broadcast_multiply_fusion = (f32[6144,16]{1,0:T(8,128)}, f32[6144,16]{1,0:T(8,128)}) fusion(f32[6144,96]{1,0:T(8,128)S(1)} %broadcast_select_fusion, f32[6,1024,16]{2,1,0:T(8,128)S(1)} %copy-done.1), kind=kLoop, calls=%fused_computation.23 | loop fusion | flops 491520 | bytes 1572864 | tf_op jit(solution)/shard_map/mul | solution.py:110
  98.0 2.1 copy.36
  100.1 3.4 %reshape.164 = f32[6,1024,16,5]{1,0,3,2:T(8,128)} reshape(f32[6144,80]{0,1:T(8,128)} %copy.36) | data formatting | bytes 3932160 | tf_op jit(solution)/shard_map/reshape | solution.py:106
  103.5 3.2 %copy.38 = f32[6,1024,16]{1,2,0:T(8,128)} copy(f32[6,1024,16]{2,1,0:T(8,128)} %bitcast.89) | data formatting | bytes 786432 | tf_op jit(solution)/shard_map/mul | solution.py:110
  106.7 3.0 %copy.35 = f32[6,1024,16]{1,2,0:T(8,128)} copy(f32[6,1024,16]{2,1,0:T(8,128)} %bitcast.88) | data formatting | bytes 786432 | tf_op jit(solution)/shard_map/mul | solution.py:110
  109.7 0.0 copy-done.8
  109.7 7.4 %multiply_add_fusion = (f32[5,64,1024]{2,1,0:T(8,128)}, f32[5,64,1024]{2,1,0:T(8,128)}) fusion(f32[5,64,1024]{2,1,0:T(8,128)S(1)} %copy-done.5, f32[64,16,6,1]{0,1,3,2:T(8,128)} %constant.157, f32[6,1024,16,5]{1,2,3,0:T(8,128)S(1)} %copy-done.3, f32[6,1024,16,5]{1,0,3,2:T(8,128)} %reshape.164, f32[6,1024,16]{1,2,0:T(8,128)} %copy.40, ...), kind=kOutput, calls=%fused_computation.30 | convolution fusion | flops 382238720 | bytes 10641408 | tf_op jit(solution)/shard_map/pqf,feqv->vpe/dot_general | solution.py:113
  117.1 1.8 copy.41
  118.9 34.8 %gather_fusion.2 = f32[8192,320]{1,0:T(8,128)} fusion(f32[1024,320]{1,0:T(8,128)S(1)} %copy.41, s32[8192]{0:T(1024)} %fusion.29), kind=kCustom, calls=%fused_computation.2 | custom fusion | bytes 21004288 | tf_op jit(solution)/shard_map/jit(_take)/gather | solution.py:131
  153.7 12.1 %copy.42 = f32[8192,320]{0,1:T(8,128)} copy(f32[8192,320]{1,0:T(8,128)} %gather_fusion.2) | data formatting | bytes 20971520 | tf_op jit(solution)/shard_map/jit(_take)/gather | solution.py:131
  165.7 5.7 %multiply_reduce_fusion = f32[8192,5]{0,1:T(8,128)S(1)} fusion(f32[8192,5,64]{0,2,1:T(8,128)} %bitcast.85, f32[8192,64]{0,1:T(8,128)S(1)} %bitcast.91, pred[8192]{0:T(1024)(128)(4,1)S(1)} %compare_and_fusion), kind=kLoop, calls=%fused_computation.5 | loop fusion | flops 7823360 | bytes 12754944
  171.4 2.6 %copy.53 = f32[8192,5]{1,0:T(8,128)} copy(f32[8192,5]{0,1:T(8,128)S(1)} %multiply_reduce_fusion) | data formatting | bytes 327680 | tf_op jit(solution)/shard_map/rvp,pr->rv/dot_general | solution.py:132
  174.1 24.5 %scatter_custom_fusion.1 = f32[16384,5]{1,0:T(8,128)} fusion(s32[8192]{0:T(1024)} %bitcast.103, f32[8192,5]{1,0:T(8,128)} %copy.53, f32[]{:T(128)} %constant.121.clone.1), kind=kCustom, calls=%fused_computation.6 | custom fusion | bytes 328192 | tf_op jit(solution)/shard_map/scatter | solution.py:166
  198.6 5.2 %copy.43 = f32[8,2048,5]{1,2,0:T(8,128)S(1)} copy(f32[8,2048,5]{2,1,0:T(8,128)} %bitcast.86) | data formatting | bytes 655360 | tf_op jit(solution)/shard_map/all_to_all | solution.py:167
  203.8 20.9 %all_to_all.12 = f32[8,2048,5]{1,2,0:T(8,128)S(1)} all-to-all(f32[8,2048,5]{1,2,0:T(8,128)S(1)} %copy.43), channel_id=1, replica_groups=mesh['valve'=4,'bulk'=8] {'bulk'}, dimensions={0} | all-to-all | bytes 655360 | tf_op jit(solution)/shard_map/all_to_all | solution.py:167
  224.7 0.8 copy.72
  (28 shorter events, 0.1 us)
Async XLA Ops:
  0.6 27.7 %copy-start.15 = (f32[16,6,64,1]{2,0,3,1:T(8,128)S(1)}, f32[16,6,64,1]{2,0,3,1:T(8,128)}, u32[]{:S(2)}) copy-start(f32[16,6,64,1]{2,0,3,1:T(8,128)} %constant.156) | copy-start | bytes 73732
  28.3 11.1 %copy-start = (f32[6,1024,16]{2,1,0:T(8,128)}, f32[6,1024,16]{2,1,0:T(8,128)S(1)}, u32[]{:S(2)}) copy-start(f32[6,1024,16]{2,1,0:T(8,128)S(1)} %copy.32) | copy-start | bytes 1179652
  32.3 3.7 %copy-start.2 = (f32[6,1024,16,5]{1,2,3,0:T(8,128)}, f32[6,1024,16,5]{1,2,3,0:T(8,128)S(1)}, u32[]{:S(2)}) copy-start(f32[6,1024,16,5]{1,2,3,0:T(8,128)S(1)} %convolution_bitcast_fusion) | copy-start | bytes 5898244
  39.4 10.2 %copy-start.11 = (s32[6,1024]{1,0:T(8,128)S(1)}, s32[6,1024]{1,0:T(8,128)}, u32[]{:S(2)}) copy-start(s32[6,1024]{1,0:T(8,128)} %param.15) | copy-start | bytes 73732
  39.4 10.2 %copy-start.12 = (s32[8192]{0:T(1024)S(1)}, s32[8192]{0:T(1024)}, u32[]{:S(2)}) copy-start(s32[8192]{0:T(1024)} %param.16) | copy-start | bytes 98308
  39.4 10.9 %copy-start.9 = (s32[8192,1]{0,1:T(1,128)S(1)}, s32[8192,1]{0,1:T(1,128)}, u32[]{:S(2)}) copy-start(s32[8192,1]{0,1:T(1,128)} %param.18) | copy-start | bytes 98308
  43.9 10.4 %copy-start.14 = (f32[3,8192]{1,0:T(4,128)S(1)}, f32[3,8192]{1,0:T(4,128)}, u32[]{:S(2)}) copy-start(f32[3,8192]{1,0:T(4,128)} %param.17) | copy-start | bytes 294916
  47.2 17.6 %collective-permute-start.1 = (f32[64,96]{1,0:T(8,128)}, f32[64,96]{1,0:T(8,128)}, u32[]{:S(2)}, u32[]{:S(2)}) collective-permute-start(f32[64,96]{1,0:T(8,128)} %get-tuple-element.17), channel_id=1, source_target_pairs={{8,0},{16,8},{24,16},{0,24},{9,1},{17,9},{25,17},{1,25},{10,2},{18... | collective-permute-start | bytes 73736 | tf_op jit(solution)/shard_map/ppermute | solution.py:20
  49.6 15.2 %collective-permute-start = (f32[64,96]{1,0:T(8,128)}, f32[64,96]{1,0:T(8,128)}, u32[]{:S(2)}, u32[]{:S(2)}) collective-permute-start(f32[64,96]{1,0:T(8,128)} %get-tuple-element.16), channel_id=1, source_target_pairs={{0,8},{8,16},{16,24},{24,0},{1,9},{9,17},{17,25},{25,1},{2,10},{10... | collective-permute-start | bytes 73736 | tf_op jit(solution)/shard_map/ppermute | solution.py:19
  52.8 3.4 %copy-start.4 = (f32[5,64,1024]{2,1,0:T(8,128)S(1)}, f32[5,64,1024]{2,1,0:T(8,128)}, u32[]{:S(2)}) copy-start(f32[5,64,1024]{2,1,0:T(8,128)} %param.11) | copy-start | bytes 3932164
  52.8 3.4 %copy-start.13 = (f32[3,64,64,1]{2,1,3,0:T(8,128)S(1)}, f32[3,64,64,1]{2,1,3,0:T(8,128)}, u32[]{:S(2)}) copy-start(f32[3,64,64,1]{2,1,3,0:T(8,128)} %constant.155) | copy-start | bytes 147460
  55.4 6.0 %copy-start.7 = (f32[16,6,1024]{2,1,0:T(8,128)S(1)}, f32[16,6,1024]{2,1,0:T(8,128)}, u32[]{:S(2)}) copy-start(f32[16,6,1024]{2,1,0:T(8,128)} %reshape.160) | copy-start | bytes 1179652
  55.7 6.7 %copy-start.10 = (f32[64,1024]{1,0:T(8,128)S(1)}, f32[64,1024]{1,0:T(8,128)}, u32[]{:S(2)}) copy-start(f32[64,1024]{1,0:T(8,128)} %param.13) | copy-start | bytes 786436
  89.7 4.8 %copy-start.1 = (f32[6,1024,16]{2,1,0:T(8,128)S(1)}, f32[6,1024,16]{2,1,0:T(8,128)}, u32[]{:S(2)}) copy-start(f32[6,1024,16]{2,1,0:T(8,128)} %copy-done) | copy-start | bytes 1179652
  103.5 6.2 %copy-start.3 = (f32[6,1024,16,5]{1,2,3,0:T(8,128)S(1)}, f32[6,1024,16,5]{1,2,3,0:T(8,128)}, u32[]{:S(2)}) copy-start(f32[6,1024,16,5]{1,2,3,0:T(8,128)} %copy-done.2) | copy-start | bytes 5898244
  103.5 6.2 %copy-start.5 = (f32[5,64,1024]{2,1,0:T(8,128)S(1)}, f32[5,64,1024]{2,1,0:T(8,128)}, u32[]{:S(2)}) copy-start(f32[5,64,1024]{2,1,0:T(8,128)} %param.11) | copy-start | bytes 3932164
  103.5 6.2 %copy-start.8 = (f32[64,1024]{1,0:T(8,128)S(1)}, f32[64,1024]{1,0:T(8,128)}, u32[]{:S(2)}) copy-start(f32[64,1024]{1,0:T(8,128)} %neg.4) | copy-start | bytes 786436
  153.6 12.1 %copy-start.6 = (f32[64,8192]{1,0:T(8,128)S(1)}, f32[64,8192]{1,0:T(8,128)}, u32[]{:S(2)}) copy-start(f32[64,8192]{1,0:T(8,128)} %mul.259) | copy-start | bytes 6291460
where the time goes:
time: 227 us; the launch traced here: 226 us
  local copies, waits for them, and re-layouts  155 us (68%)
  other arithmetic  29.2 us (13%)
  blocking collectives  20.9 us (9%)
  matrix products  16.6 us (7%)
  starting transfers between devices  2.41 us (1%)
    gather x2, local copies, waits for them, and re-layouts, receptor_rows(): jnp.take(element_rows, donors, axis=0).reshape(donors.shape[0], nvars, 64)  46.8 us
    scatter x1, local copies, waits for them, and re-layouts, on_device(): outgoing_slots = outgoing_slots.at[places].set(receptor_vals)  24.5 us
    scatter x1, local copies, waits for them, and re-layouts, rim_rows(): senders = jnp.zeros((2 * rim_count,), jnp.int32).at[slots].set(jnp.arange...  23 us
    gather x1, local copies, waits for them, and re-layouts, surface_term(): outer = jnp.take(full_table, links, axis=0)  21.1 us
    all_to_all x1, blocking collectives, on_device(): lax.all_to_all(outgoing_slots, 'bulk', split_axis=0, concat_axis=0, tiled...  20.9 us
    dot_general x1, matrix products, surface_term(): jnp.einsum('pqf,feqv->vpe', lift_faces, jump_term, precision=lax.Precisio...  7.4 us
    unnamed x2, other arithmetic  5.83 us
    all_to_all x1, local copies, waits for them, and re-layouts, on_device(): lax.all_to_all(outgoing_slots, 'bulk', split_axis=0, concat_axis=0, tiled...  5.22 us
  transfers between devices with their start and end apart: 2, of which 0 were waited for; matrix products, arithmetic and copies ran while one was open for 7% of the time, Pallas kernels for 0%

commit v1 on v0

v1 whole, which is shorter than its diff:
```python
import functools

import jax
import jax.numpy as jnp
import numpy as np
from jax import lax
from jax.experimental import pallas as pl
from jax.experimental.pallas import tpu as pltpu
from jax.sharding import PartitionSpec as P

gauss_nodes = (-0.8611363115940526, -0.3399810435848563, 0.3399810435848563, 0.8611363115940526)
quad_weights = (0.3478548451374538, 0.6521451548625461, 0.6521451548625461, 0.3478548451374538)
section_step = 0.2
MESH = pl.DeviceIdType.MESH
VMEM_BYTES = 48 * 1024 * 1024


def lagrange_at(x):
    values = []
    for j in range(4):
        factor = 1.0
        for m in range(4):
            if m != j:
                factor = factor * (x - gauss_nodes[m]) * (1.0 / (gauss_nodes[j] - gauss_nodes[m]))
        values.append(factor)
    return values


def tables():
    slopes = np.zeros((4, 4))
    for i in range(4):
        for j in range(4):
            summed = 0.0
            for m in range(4):
                if m != j:
                    product = 1.0 / (gauss_nodes[j] - gauss_nodes[m])
                    for n in range(4):
                        if n != j and n != m:
                            product = (
                                product
                                * (gauss_nodes[i] - gauss_nodes[n])
                                / (gauss_nodes[j] - gauss_nodes[n])
                            )
                    summed = summed + product
            slopes[i, j] = summed
    end_values = [lagrange_at(-1.0), lagrange_at(1.0)]
    extrapolate = np.zeros((96, 64))
    lifting = np.zeros((64, 96))
    derivative = np.zeros((3, 64, 64))
    for p in range(64):
        point_idx = (p // 16, p // 4 % 4, p % 4)
        for f in range(6):
            normal_dir = f // 2
            across = [t for t in range(3) if t != normal_dir]
            q = point_idx[across[0]] * 4 + point_idx[across[1]]
            flux_row = f * 16 + q
            extrapolate[flux_row, p] = end_values[f % 2][point_idx[normal_dir]]
            lifting[p, flux_row] = (
                end_values[f % 2][point_idx[normal_dir]] / quad_weights[point_idx[normal_dir]]
            )
        for s in range(64):
            other_idx = (s // 16, s // 4 % 4, s % 4)
            for normal_dir in range(3):
                if all((point_idx[t] == other_idx[t] for t in range(3) if t != normal_dir)):
                    derivative[normal_dir, p, s] = slopes[
                        point_idx[normal_dir], other_idx[normal_dir]
                    ]
    return extrapolate, derivative, lifting


def split_columns(matrix):
    matrix = np.asarray(matrix, np.float32)
    hi = matrix.astype(jnp.bfloat16)
    lo = (matrix - hi.astype(np.float32)).astype(jnp.bfloat16)
    return jnp.asarray(np.concatenate([hi, hi, lo], axis=1))


def halves(x):
    hi = x.astype(jnp.bfloat16)
    lo = (x - hi.astype(jnp.float32)).astype(jnp.bfloat16)
    return hi, lo


def split_rows(x):
    hi, lo = halves(x)
    return jnp.concatenate([hi, lo, hi], axis=0)


def dot(a, b):
    return jnp.dot(a, b, preferred_element_type=jnp.float32)


def dot_nt(a, b):
    return lax.dot_general(a, b, (((1,), (1,)), ((), ())), preferred_element_type=jnp.float32)


def by_face(speed_ref, tiles):
    count = tiles.shape[0]
    for t in range(count):
        tiles[t] = speed_ref[:, 128 * t : 128 * t + 128]
    return [
        jnp.concatenate([tiles[t, pl.ds(f, 16, stride=6), :] for t in range(count)], axis=1)
        for f in range(6)
    ]


def table_kernel(
    sol_ref, speed_ref, links_ref, ext_ref, table_ref, nat, tiles, out_rows, in_rows, send_sem, recv_sem
):
    nvars, _, elems = sol_ref.shape
    faces_total = 6 * elems
    rim = in_rows.shape[0] // 2
    size = lax.axis_size("valve")
    me = lax.axis_index("valve")
    up, down = lax.rem(me + 1, size), lax.rem(me + size - 1, size)
    barrier = pltpu.get_barrier_semaphore()
    for peer in (up, down):
        pl.semaphore_signal(barrier, inc=1, device_id={"valve": peer}, device_id_type=MESH)
    ext = ext_ref[...]
    speeds = by_face(speed_ref, tiles)
    for v in range(nvars):
        vals = dot(ext, split_rows(sol_ref[v]))
        for f in range(6):
            nat[f, 16 * v : 16 * v + 16, :] = vals[16 * f : 16 * f + 16]
    picked = jnp.zeros((2 * rim, 128), jnp.float32)
    slot = lax.broadcasted_iota(jnp.int32, (2 * rim, elems), 0) + faces_total
    for f in range(6):
        nat[f, 16 * nvars : 16 * nvars + 16, :] = speeds[f]
        nat[f, 16 * nvars + 16 :, :] = jnp.zeros((112 - 16 * nvars, elems), jnp.float32)
        rows = nat[f].T
        table_ref[f * elems : (f + 1) * elems, :] = rows
        onehot = (links_ref[f : f + 1, :] == slot).astype(jnp.float32).astype(jnp.bfloat16)
        hi, lo = halves(rows)
        picked = picked + dot(onehot, hi) + dot(onehot, lo)
    out_rows[...] = picked
    pl.semaphore_wait(barrier, 2)
    to_up = pltpu.make_async_remote_copy(
        src_ref=out_rows.at[rim:],
        dst_ref=in_rows.at[:rim],
        send_sem=send_sem.at[0],
        recv_sem=recv_sem.at[0],
        device_id={"valve": up},
        device_id_type=MESH,
    )
    to_down = pltpu.make_async_remote_copy(
        src_ref=out_rows.at[:rim],
        dst_ref=in_rows.at[rim:],
        send_sem=send_sem.at[1],
        recv_sem=recv_sem.at[1],
        device_id={"valve": down},
        device_id_type=MESH,
    )
    to_up.start()
    to_down.start()
    to_up.wait()
    to_down.wait()
    table_ref[faces_total:, :] = in_rows[...]


def face_table(solution, face_speed, face_link, extrapolate):
    elems = solution.shape[2]
    rim = elems // 16
    vmem = pl.BlockSpec(memory_space=pltpu.VMEM)
    return pl.pallas_call(
        table_kernel,
        out_shape=jax.ShapeDtypeStruct((6 * elems + 2 * rim, 128), jnp.float32),
        in_specs=[vmem] * 4,
        out_specs=vmem,
        scratch_shapes=[
            pltpu.VMEM((6, 128, elems), jnp.float32),
            pltpu.VMEM((elems // 128, 96, 128), jnp.float32),
            pltpu.VMEM((2 * rim, 128), jnp.float32),
            pltpu.VMEM((2 * rim, 128), jnp.float32),
            pltpu.SemaphoreType.DMA((2,)),
            pltpu.SemaphoreType.DMA((2,)),
        ],
        compiler_params=pltpu.CompilerParams(
            collective_id=0, has_side_effects=True, vmem_limit_bytes=VMEM_BYTES
        ),
        name="face_table",
    )(solution, face_speed, face_link, extrapolate)


def section_kernel(
    links_ref, table_ref, sol_ref, vel_ref, jac_ref, speed_ref, ops_ref, lift_ref,
    rate_ref, hi_ref, lo_ref, rows, jump, tiles,
):
    nvars, _, width = sol_ref.shape
    start = pl.program_id(0) * width
    step = 16

    def gather(i, carry):
        base = pl.multiple_of(i * step, step)
        for f in range(6):
            for u in range(step):
                link = links_ref[f, start + base + u]
                rows[f, pl.ds(base + u, 1), :] = table_ref[pl.ds(link, 1), :]
        return carry

    lax.fori_loop(0, width // step, gather, 0)
    ops = ops_ref[...]
    vel = vel_ref[...]
    speeds = by_face(speed_ref, tiles)
    own = [dot(ops, split_rows(sol_ref[v])) for v in range(nvars)]
    for f in range(6):
        outer = rows[f].T
        speed = speeds[f]
        normal = 0.5 * (speed - outer[16 * nvars : 16 * nvars + 16])
        mean, diff = 0.5 * normal, 0.5 * jnp.abs(normal)
        for v in range(nvars):
            inner = own[v][16 * f : 16 * f + 16]
            other = outer[16 * v : 16 * v + 16]
            jump[v, 16 * f : 16 * f + 16, :] = (
                mean * (inner + other) + diff * (inner - other) - speed * inner
            )
    lift = lift_ref[...]
    jac = jac_ref[...]
    for v in range(nvars):
        total = dot(lift, split_rows(jump[v]))
        for d in range(3):
            total = total + vel[d : d + 1] * own[v][96 + 64 * d : 160 + 64 * d]
        rate = -jac * total
        rate_ref[v] = rate
        hi, lo = halves(sol_ref[v] + section_step * rate)
        hi_ref[64 * v : 64 * v + 64, :] = hi
        lo_ref[64 * v : 64 * v + 64, :] = lo


def section(face_link, table, solution, velocity, inv_jacobian, face_speed, operators, lifting):
    nvars, points, elems = solution.shape
    width = 256
    whole = lambda shape: pl.BlockSpec(shape, lambda i, links: (0,) * len(shape))
    block = lambda rows: pl.BlockSpec((rows, width), lambda i, links: (0, i))
    cube = pl.BlockSpec((nvars, points, width), lambda i, links: (0, 0, i))
    pieces = jax.ShapeDtypeStruct((nvars * points, elems), jnp.bfloat16)
    return pl.pallas_call(
        section_kernel,
        grid_spec=pltpu.PrefetchScalarGridSpec(
            num_scalar_prefetch=1,
            grid=(elems // width,),
            in_specs=[
                whole(table.shape), cube, block(3), block(64), block(96),
                whole(operators.shape), whole(lifting.shape),
            ],
            out_specs=[cube, block(nvars * points), block(nvars * points)],
            scratch_shapes=[
                pltpu.VMEM((6, width, 128), jnp.float32),
                pltpu.VMEM((nvars, 96, width), jnp.float32),
                pltpu.VMEM((width // 128, 96, 128), jnp.float32),
            ],
        ),
        out_shape=[jax.ShapeDtypeStruct(solution.shape, jnp.float32), pieces, pieces],
        compiler_params=pltpu.CompilerParams(vmem_limit_bytes=VMEM_BYTES),
        name="section",
    )(face_link, table, solution, velocity, inv_jacobian, face_speed, operators, lifting)


def receptor_kernel(buckets, nvars, hi_ref, lo_ref, donor_ref, coord_ref, owner_ref, out_ref, pieces, acc, seen, upper):
    elems = hi_ref.shape[1]
    width = donor_ref.shape[1]
    capacity = 16384 // buckets
    step = pl.program_id(0)
    rows = nvars * 64

    @pl.when(step == 0)
    def _():
        pieces[:rows, :] = hi_ref[...]
        pieces[rows:, :] = lo_ref[...]
        seen[...] = jnp.zeros_like(seen)
        upper[...] = (
            lax.broadcasted_iota(jnp.int32, (width, width), 0)
            < lax.broadcasted_iota(jnp.int32, (width, width), 1)
        ).astype(jnp.float32).astype(jnp.bfloat16)

    donor = donor_ref[...]
    chosen = (lax.broadcasted_iota(jnp.int32, (elems, width), 0) == donor)
    chosen = chosen.astype(jnp.float32).astype(jnp.bfloat16)
    picked = dot(pieces[...], chosen)
    lx = lagrange_at(coord_ref[0:1, :])
    ly = lagrange_at(coord_ref[1:2, :])
    lz = jnp.concatenate(lagrange_at(coord_ref[2:3, :]), axis=0)
    yz = jnp.concatenate([ly[j] * lz for j in range(4)], axis=0)
    weights = jnp.concatenate([lx[i] * yz for i in range(4)], axis=0)
    values = []
    for v in range(nvars):
        both = picked[64 * v : 64 * v + 64] + picked[rows + 64 * v : rows + 64 * v + 64]
        values.append(jnp.sum(both * weights, axis=0, keepdims=True))

    owner = owner_ref[...]
    named = (lax.broadcasted_iota(jnp.int32, (16, width), 0) == owner).astype(jnp.float32)
    before = dot(named.astype(jnp.bfloat16), upper[...]) + seen[:, 0:1]
    rank = jnp.sum(named * before, axis=0, keepdims=True)
    seen[...] = seen[...] + jnp.sum(named, axis=1, keepdims=True)
    place = owner * capacity + rank.astype(jnp.int32)
    in_row = (lax.broadcasted_iota(jnp.int32, (64, width), 0) == place // 256)
    in_row = in_row.astype(jnp.float32).astype(jnp.bfloat16)
    in_lane = (lax.broadcasted_iota(jnp.int32, (256, width), 0) == lax.rem(place, 256))
    in_lane = in_lane.astype(jnp.float32).astype(jnp.bfloat16)
    parts = []
    for v in range(nvars):
        for piece in halves(values[v]):
            parts.append(in_row * piece)
    spread = dot_nt(jnp.concatenate(parts, axis=0), in_lane)
    acc[...] = jnp.where(step == 0, 0.0, acc[...]) + spread

    @pl.when(step == pl.num_programs(0) - 1)
    def _():
        for v in range(nvars):
            both = acc[128 * v : 128 * v + 64, :] + acc[128 * v + 64 : 128 * v + 128, :]
            out_ref[pl.ds(v, 64, stride=2 * nvars), :] = both[:, :128]
            out_ref[pl.ds(nvars + v, 64, stride=2 * nvars), :] = both[:, 128:]


def receptor_slots(hi, lo, donors, coords, owners, buckets):
    rows, elems = hi.shape
    nvars = rows // 64
    receptors = donors.shape[1]
    width = 512
    whole = pl.BlockSpec((rows, elems), lambda i: (0, 0))
    block = lambda count: pl.BlockSpec((count, width), lambda i: (0, i))
    return pl.pallas_call(
        functools.partial(receptor_kernel, buckets, nvars),
        grid=(receptors // width,),
        in_specs=[whole, whole, block(1), block(3), block(1)],
        out_specs=pl.BlockSpec((nvars * 128, 128), lambda i: (0, 0)),
        out_shape=jax.ShapeDtypeStruct((nvars * 128, 128), jnp.float32),
        scratch_shapes=[
            pltpu.VMEM((2 * rows, elems), jnp.bfloat16),
            pltpu.VMEM((128 * nvars, 256), jnp.float32),
            pltpu.VMEM((16, 128), jnp.float32),
            pltpu.VMEM((width, width), jnp.bfloat16),
        ],
        compiler_params=pltpu.CompilerParams(vmem_limit_bytes=VMEM_BYTES),
        name="receptor_slots",
    )(hi, lo, donors, coords, owners)


def exchange_kernel(buckets, nvars, send_ref, out_ref, held, send_sem, recv_sem):
    block = nvars * 128 // buckets
    me = lax.axis_index("bulk")
    barrier = pltpu.get_barrier_semaphore()
    peers = [lax.rem(me + k, buckets) for k in range(1, buckets)]
    for peer in peers:
        pl.semaphore_signal(barrier, inc=1, device_id={"bulk": peer}, device_id_type=MESH)
    pl.semaphore_wait(barrier, buckets - 1)
    mine = pl.ds(pl.multiple_of(me * block, 8), block)
    copies = []
    for k, peer in enumerate(peers):
        copy = pltpu.make_async_remote_copy(
            src_ref=send_ref.at[pl.ds(pl.multiple_of(peer * block, 8), block)],
            dst_ref=held.at[mine],
            send_sem=send_sem.at[k],
            recv_sem=recv_sem.at[k],
            device_id={"bulk": peer},
            device_id_type=MESH,
        )
        copy.start()
        copies.append(copy)
    held[mine, :] = send_ref[mine, :]
    for copy in copies:
        copy.wait()
    for j in range(128):
        out_ref[:, 128 * j : 128 * j + 128] = held[nvars * j : nvars * j + nvars, :]


def exchange(slots, nvars, buckets):
    vmem = pl.BlockSpec(memory_space=pltpu.VMEM)
    return pl.pallas_call(
        functools.partial(exchange_kernel, buckets, nvars),
        out_shape=jax.ShapeDtypeStruct((nvars, 16384), jnp.float32),
        in_specs=[vmem],
        out_specs=vmem,
        scratch_shapes=[
            pltpu.VMEM(slots.shape, jnp.float32),
            pltpu.SemaphoreType.DMA((buckets - 1,)),
            pltpu.SemaphoreType.DMA((buckets - 1,)),
        ],
        compiler_params=pltpu.CompilerParams(
            collective_id=1, has_side_effects=True, vmem_limit_bytes=VMEM_BYTES
        ),
        name="exchange",
    )(slots)


def on_device(
    solution, velocity, inv_jacobian, face_speed, face_link, donor_elem, ref_coords, owner_list
):
    extrapolate, derivative, lifting = tables()
    nvars = solution.shape[0]
    buckets = lax.axis_size("bulk")
    operators = np.concatenate([extrapolate, derivative.reshape(192, 64)], axis=0)
    table = face_table(solution, face_speed, face_link, split_columns(extrapolate))
    section_rate, hi, lo = section(
        face_link, table, solution, velocity, inv_jacobian, face_speed,
        split_columns(operators), split_columns(lifting),
    )
    slots = receptor_slots(
        hi, lo, donor_elem.reshape(1, -1), ref_coords, owner_list.reshape(1, -1), buckets
    )
    return (section_rate, exchange(slots, nvars, buckets))


def solution(mesh):
    placed = (
        P(None, None, ("valve", "bulk")),
        P(None, ("valve", "bulk")),
        P(None, ("valve", "bulk")),
        P(None, ("valve", "bulk")),
        P(None, ("valve", "bulk")),
        P(("valve", "bulk")),
        P(None, ("valve", "bulk")),
        P(("valve", "bulk"), None),
    )
    return jax.shard_map(
        on_device,
        mesh=mesh,
        in_specs=placed,
        out_specs=(P(None, None, ("valve", "bulk")), P(None, ("valve", "bulk"))),
        check_vma=False,
    )
```

time: 227 us -> 67.9 us (0.30)
  local copies, waits for them, and re-layouts: 155 us -> 6.36 us
  Pallas kernels: 0 us -> 60.3 us
  other arithmetic: 29.2 us -> 0 us
  blocking collectives: 20.9 us -> 0 us
  matrix products: 16.6 us -> 0 us
  starting transfers between devices: 2.41 us -> 0 us
    gather x4 -> x0, local copies, waits for them, and re-layouts: 70.5 us -> none  [the longest x2 46.8 us: receptor_rows(): jnp.take(element_rows, donors, axis=0).reshape(donors.shape[0], nvars, 64)]
    pallas_call x0 -> x4, Pallas kernels: none -> 60.3 us  [the longest x1 26.4 us: receptor_slots(): pl.pallas_call(functools.partial(receptor_kernel, buckets, nvars), grid=(...]
    scatter x2 -> x0, local copies, waits for them, and re-layouts: 47.5 us -> none  [the longest x1 24.5 us: on_device(): outgoing_slots = outgoing_slots.at[places].set(receptor_vals)]
    all_to_all x1 -> x0, blocking collectives: 20.9 us -> none  [on_device(): lax.all_to_all(outgoing_slots, 'bulk', split_axis=0, concat_axis=0, tiled...]
    dot_general x3 -> x0, matrix products: 16.6 us -> none  [the longest x1 7.4 us: surface_term(): jnp.einsum('pqf,feqv->vpe', lift_faces, jump_term, precision=lax.Precisio...]
    concatenate x2 -> x0, other arithmetic: 8.24 us -> none  [the longest x1 4.48 us: on_device(): jnp.concatenate([values.reshape(faces_total, 16 * nvars), speeds], axis=1)]
    mul x3 -> x0, local copies, waits for them, and re-layouts: 7.87 us -> none  [the longest x1 3.16 us: surface_term(): 0.5 * jnp.abs(normal) * (values - outer_vals)]
    reshape x4 -> x0, local copies, waits for them, and re-layouts: 7.01 us -> none  [the longest x1 3.39 us: surface_term(): outer_vals = outer[:, :16 * nvars].reshape(6 * elems, 16, nvars)]
  transfers between devices with their start and end apart: 2 -> 0, of which waited for: 0 -> 0; matrix products, arithmetic and copies ran while one was open for 7% -> 0% of each run, Pallas kernels for 0% -> 0%
where the time goes in v1:
time: 67.9 us; the launch traced here: 67.3 us
  Pallas kernels  60.3 us (89%)
  local copies, waits for them, and re-layouts  6.36 us (9%)
  between operations  0.71 us (1%)
    pallas_call x1, Pallas kernels, receptor_slots(): pl.pallas_call(functools.partial(receptor_kernel, buckets, nvars), grid=(...  26.4 us
    pallas_call x1, Pallas kernels, section(): pl.pallas_call(section_kernel, grid_spec=pltpu.PrefetchScalarGridSpec(num...  17.1 us
    pallas_call x1, Pallas kernels, exchange(): pl.pallas_call(functools.partial(exchange_kernel, buckets, nvars), out_sh...  11.1 us
    unnamed x25, local copies, waits for them, and re-layouts  6.36 us
    pallas_call x1, Pallas kernels, face_table(): pl.pallas_call(table_kernel, out_shape=jax.ShapeDtypeStruct((6 * elems +...  5.63 us

profile of v1, /device:TPU:0, one launch (start us, length us, event | category | flops | bytes accessed | tf_op | source)
XLA Modules:
  0.0 67.3 jit_solution(11590691540542200790)
XLA Ops:
  0.6 0.0 copy-start.1
  0.6 1.3 %copy-done.1 = f32[5,64,1024]{2,1,0:T(8,128)S(1)} copy-done((f32[5,64,1024]{2,1,0:T(8,128)S(1)}, f32[5,64,1024]{2,1,0:T(8,128)}, u32[]{:S(2)}) %copy-start.1) | copy-done | bytes 1310744
  1.9 0.0 copy-start.2
  2.0 1.0 %copy-done.2 = f32[96,1024]{1,0:T(8,128)S(1)} copy-done((f32[96,1024]{1,0:T(8,128)S(1)}, f32[96,1024]{1,0:T(8,128)}, u32[]{:S(2)}) %copy-start.2) | copy-done | bytes 393240
  2.9 0.0 copy-start.5
  2.9 0.8 %copy-done.5 = s32[6,1024]{1,0:T(8,128)S(1)} copy-done((s32[6,1024]{1,0:T(8,128)S(1)}, s32[6,1024]{1,0:T(8,128)}, u32[]{:S(2)}) %copy-start.5) | copy-done | bytes 24600
  3.7 0.0 copy-start.7
  3.7 0.8 %copy-done.7 = bf16[96,192]{1,0:T(8,128)(2,1)S(1)} copy-done((bf16[96,192]{1,0:T(8,128)(2,1)S(1)}, bf16[96,192]{1,0:T(8,128)(2,1)}, u32[]{:S(2)}) %copy-start.7) | copy-done | bytes 36888
  4.5 0.0 copy-start.3
  4.5 0.0 copy-start.4
  4.5 0.0 copy-start.8
  4.5 0.0 copy-start.11
  4.5 5.6 %face_table.1.table_ref = f32[6272,128]{1,0:T(8,128)S(1)} custom-call(f32[5,64,1024]{2,1,0:T(8,128)S(1)} %copy-done.1, f32[96,1024]{1,0:T(8,128)S(1)} %copy-done.2, s32[6,1024]{1,0:T(8,128)S(1)} %copy-done.5, bf16[96,192]{1,0:T(8,128)(2,1)S(1)} %copy-done.7), custom_call_target="tpu_custom_call" | custom-call | tf_op jit(solution)/shard_map/face_table/pallas_call | solution.py:164
  10.2 0.0 copy-start
  10.2 1.7 %copy-done = f32[6272,128]{1,0:T(8,128)} copy-done((f32[6272,128]{1,0:T(8,128)}, f32[6272,128]{1,0:T(8,128)S(1)}, u32[]{:S(2)}) %copy-start) | copy-done | bytes 3211288
  11.8 0.0 copy-done.3
  11.8 0.0 copy-done.4
  11.8 0.0 copy-done.8
  11.8 0.0 copy-done.11
  11.8 0.0 copy-start.6
  11.9 0.0 copy-start.9
  11.9 0.0 copy-start.10
  11.9 17.1 %section.1 = (f32[5,64,1024]{2,1,0:T(8,128)}, bf16[320,1024]{1,0:T(8,128)(2,1)S(1)}, bf16[320,1024]{1,0:T(8,128)(2,1)S(1)}) custom-call(s32[6,1024]{1,0:T(8,128)S(1)} %copy-done.5, f32[6272,128]{1,0:T(8,128)} %copy-done, f32[5,64,1024]{2,1,0:T(8,128)S(1)} %copy-done.1, f32[3,1024]{1,0:T(4,128)S(1)} %copy-done.11, f32[64,1024]{1,0:T(8,128)S(1)} %copy-done.3, ...), custom_call_target="tpu_custom_call" | custom-call | tf_op jit(solution)/shard_map/section/pallas_call | solution.py:236
  28.9 0.0 copy-done.6
  28.9 0.0 copy-done.9
  28.9 0.0 copy-done.10
  28.9 26.4 %receptor_slots.1.send_ref = f32[640,128]{1,0:T(8,128)S(1)} custom-call(bf16[320,1024]{1,0:T(8,128)(2,1)S(1)} %get-tuple-element.6.hi_ref, bf16[320,1024]{1,0:T(8,128)(2,1)S(1)} %get-tuple-element.7.lo_ref, s32[1,8192]{1,0:T(1,128)S(1)} %bitcast.2, f32[3,8192]{1,0:T(4,128)S(1)} %copy-done.6, s32[1,8192]{1,0:T(1,128)S(1)} %bitcast.3), custom_call_target="tpu_custom_call" | custom-call | tf_op jit(solution)/shard_map/receptor_slots/pallas_call | solution.py:321
  55.4 11.1 %exchange.1 = f32[5,16384]{1,0:T(8,128)S(1)} custom-call(f32[640,128]{1,0:T(8,128)S(1)} %receptor_slots.1.send_ref), custom_call_target="tpu_custom_call" | custom-call | tf_op jit(solution)/shard_map/exchange/pallas_call | solution.py:368
  66.5 0.8 %copy.14 = f32[5,16384]{1,0:T(8,128)} copy(f32[5,16384]{1,0:T(8,128)S(1)} %exchange.1) | data formatting | bytes 655360
Async XLA Ops:
  0.6 1.3 %copy-start.1 = (f32[5,64,1024]{2,1,0:T(8,128)S(1)}, f32[5,64,1024]{2,1,0:T(8,128)}, u32[]{:S(2)}) copy-start(f32[5,64,1024]{2,1,0:T(8,128)} %sol_ref.3) | copy-start | bytes 3932164
  1.9 1.0 %copy-start.2 = (f32[96,1024]{1,0:T(8,128)S(1)}, f32[96,1024]{1,0:T(8,128)}, u32[]{:S(2)}) copy-start(f32[96,1024]{1,0:T(8,128)} %speed_ref.3) | copy-start | bytes 1179652
  2.9 0.8 %copy-start.5 = (s32[6,1024]{1,0:T(8,128)S(1)}, s32[6,1024]{1,0:T(8,128)}, u32[]{:S(2)}) copy-start(s32[6,1024]{1,0:T(8,128)} %links_ref.3) | copy-start | bytes 73732
  3.7 0.8 %copy-start.7 = (bf16[96,192]{1,0:T(8,128)(2,1)S(1)}, bf16[96,192]{1,0:T(8,128)(2,1)}, u32[]{:S(2)}) copy-start(bf16[96,192]{1,0:T(8,128)(2,1)} %constant.6.clone.ext_ref) | copy-start | bytes 110596
  4.5 7.3 %copy-start.3 = (f32[64,1024]{1,0:T(8,128)S(1)}, f32[64,1024]{1,0:T(8,128)}, u32[]{:S(2)}) copy-start(f32[64,1024]{1,0:T(8,128)} %jac_ref.1) | copy-start | bytes 786436
  4.5 7.3 %copy-start.4 = (bf16[288,192]{1,0:T(8,128)(2,1)S(1)}, bf16[288,192]{1,0:T(8,128)(2,1)}, u32[]{:S(2)}) copy-start(bf16[288,192]{1,0:T(8,128)(2,1)} %constant.7.clone.ops_ref) | copy-start | bytes 331780
  4.5 7.3 %copy-start.8 = (bf16[64,288]{1,0:T(8,128)(2,1)S(1)}, bf16[64,288]{1,0:T(8,128)(2,1)}, u32[]{:S(2)}) copy-start(bf16[64,288]{1,0:T(8,128)(2,1)} %constant.8.clone.lift_ref) | copy-start | bytes 110596
  4.5 7.3 %copy-start.11 = (f32[3,1024]{1,0:T(4,128)S(1)}, f32[3,1024]{1,0:T(4,128)}, u32[]{:S(2)}) copy-start(f32[3,1024]{1,0:T(4,128)} %vel_ref.1) | copy-start | bytes 36868
  10.2 1.7 %copy-start = (f32[6272,128]{1,0:T(8,128)}, f32[6272,128]{1,0:T(8,128)S(1)}, u32[]{:S(2)}) copy-start(f32[6272,128]{1,0:T(8,128)S(1)} %face_table.1.table_ref) | copy-start | bytes 9633796
  11.8 17.1 %copy-start.6 = (f32[3,8192]{1,0:T(4,128)S(1)}, f32[3,8192]{1,0:T(4,128)}, u32[]{:S(2)}) copy-start(f32[3,8192]{1,0:T(4,128)} %coord_ref.1) | copy-start | bytes 294916
  11.9 17.1 %copy-start.9 = (s32[8192]{0:T(1024)S(1)}, s32[8192]{0:T(1024)}, u32[]{:S(2)}) copy-start(s32[8192]{0:T(1024)} %param.16) | copy-start | bytes 98308
  11.9 17.1 %copy-start.10 = (s32[8192,1]{0,1:T(1,128)S(1)}, s32[8192,1]{0,1:T(1,128)}, u32[]{:S(2)}) copy-start(s32[8192,1]{0,1:T(1,128)} %param.18) | copy-start | bytes 98308

commit v2 on v1

--- a/solution.py
+++ b/solution.py
@@ -12,7 +12,7 @@
 quad_weights = (0.3478548451374538, 0.6521451548625461, 0.6521451548625461, 0.3478548451374538)
 section_step = 0.2
 MESH = pl.DeviceIdType.MESH
-VMEM_BYTES = 48 * 1024 * 1024
+VMEM_BYTES = 56 * 1024 * 1024
 
 
 def lagrange_at(x):
@@ -105,9 +105,16 @@
 
 
 def table_kernel(
-    sol_ref, speed_ref, links_ref, ext_ref, table_ref, nat, tiles, out_rows, in_rows, send_sem, recv_sem
+    sol_hbm, speed_hbm, links_hbm, ext_ref, table_ref,
+    sol_ref, speed_ref, links_ref, nat, tiles, out_rows, in_rows, fetch_sem, send_sem, recv_sem,
 ):
     nvars, _, elems = sol_ref.shape
+    fetches = [pltpu.make_async_copy(speed_hbm, speed_ref, fetch_sem.at[nvars])]
+    for v in range(nvars):
+        fetches.append(pltpu.make_async_copy(sol_hbm.at[v], sol_ref.at[v], fetch_sem.at[v]))
+    fetches.append(pltpu.make_async_copy(links_hbm, links_ref, fetch_sem.at[nvars + 1]))
+    for fetch in fetches:
+        fetch.start()
     faces_total = 6 * elems
     rim = in_rows.shape[0] // 2
     size = lax.axis_size("valve")
@@ -117,11 +124,14 @@
     for peer in (up, down):
         pl.semaphore_signal(barrier, inc=1, device_id={"valve": peer}, device_id_type=MESH)
     ext = ext_ref[...]
+    fetches[0].wait()
     speeds = by_face(speed_ref, tiles)
     for v in range(nvars):
+        fetches[v + 1].wait()
         vals = dot(ext, split_rows(sol_ref[v]))
         for f in range(6):
             nat[f, 16 * v : 16 * v + 16, :] = vals[16 * f : 16 * f + 16]
+    fetches[nvars + 1].wait()
     picked = jnp.zeros((2 * rim, 128), jnp.float32)
     slot = lax.broadcasted_iota(jnp.int32, (2 * rim, elems), 0) + faces_total
     for f in range(6):
@@ -164,13 +174,17 @@
     return pl.pallas_call(
         table_kernel,
         out_shape=jax.ShapeDtypeStruct((6 * elems + 2 * rim, 128), jnp.float32),
-        in_specs=[vmem] * 4,
+        in_specs=[pl.BlockSpec(memory_space=pl.ANY)] * 3 + [vmem],
         out_specs=vmem,
         scratch_shapes=[
+            pltpu.VMEM(solution.shape, jnp.float32),
+            pltpu.VMEM(face_speed.shape, jnp.float32),
+            pltpu.VMEM(face_link.shape, jnp.int32),
             pltpu.VMEM((6, 128, elems), jnp.float32),
             pltpu.VMEM((elems // 128, 96, 128), jnp.float32),
             pltpu.VMEM((2 * rim, 128), jnp.float32),
             pltpu.VMEM((2 * rim, 128), jnp.float32),
+            pltpu.SemaphoreType.DMA((solution.shape[0] + 2,)),
             pltpu.SemaphoreType.DMA((2,)),
             pltpu.SemaphoreType.DMA((2,)),
         ],
@@ -183,53 +197,66 @@
 
 def section_kernel(
     links_ref, table_ref, sol_ref, vel_ref, jac_ref, speed_ref, ops_ref, lift_ref,
-    rate_ref, hi_ref, lo_ref, rows, jump, tiles,
+    rate_ref, hi_ref, lo_ref, even, odd, jump, tiles,
 ):
     nvars, _, width = sol_ref.shape
-    start = pl.program_id(0) * width
-    step = 16
-
-    def gather(i, carry):
-        base = pl.multiple_of(i * step, step)
+    half = 128
+    step = pl.program_id(0)
+    last = pl.num_programs(0) * width - half
+    ops = ops_ref[...]
+    lift = lift_ref[...]
+
+    def fetch(rows, f, u, start):
+        rows[f, pl.ds(u, 1), :] = table_ref[pl.ds(links_ref[f, start + u], 1), :]
+
+    @pl.when(step == 0)
+    def _():
+        def eight(i, carry):
+            for f in range(6):
+                for u in range(8):
+                    fetch(even, f, pl.multiple_of(8 * i, 8) + u, 0)
+            return carry
+
+        lax.fori_loop(0, half // 8, eight, 0)
+
+    def work(rows, span, coming, start):
+        vel = vel_ref[:, span]
+        jac = jac_ref[:, span]
+        tiles[...] = speed_ref[:, span]
+        sol = [sol_ref[v, :, span] for v in range(nvars)]
+        own = [dot(ops, split_rows(sol[v])) for v in range(nvars)]
         for f in range(6):
-            for u in range(step):
-                link = links_ref[f, start + base + u]
-                rows[f, pl.ds(base + u, 1), :] = table_ref[pl.ds(link, 1), :]
-        return carry
-
-    lax.fori_loop(0, width // step, gather, 0)
-    ops = ops_ref[...]
-    vel = vel_ref[...]
-    speeds = by_face(speed_ref, tiles)
-    own = [dot(ops, split_rows(sol_ref[v])) for v in range(nvars)]
-    for f in range(6):
-        outer = rows[f].T
-        speed = speeds[f]
-        normal = 0.5 * (speed - outer[16 * nvars : 16 * nvars + 16])
-        mean, diff = 0.5 * normal, 0.5 * jnp.abs(normal)
+            for u in range(half):
+                fetch(coming, f, u, start)
+            outer = rows[f].T
+            speed = tiles[pl.ds(f, 16, stride=6), :]
+            normal = 0.5 * (speed - outer[16 * nvars : 16 * nvars + 16])
+            mean, diff = 0.5 * normal, 0.5 * jnp.abs(normal)
+            for v in range(nvars):
+                inner = own[v][16 * f : 16 * f + 16]
+                other = outer[16 * v : 16 * v + 16]
+                jump[v, 16 * f : 16 * f + 16, :] = (
+                    mean * (inner + other) + diff * (inner - other) - speed * inner
+                )
         for v in range(nvars):
-            inner = own[v][16 * f : 16 * f + 16]
-            other = outer[16 * v : 16 * v + 16]
-            jump[v, 16 * f : 16 * f + 16, :] = (
-                mean * (inner + other) + diff * (inner - other) - speed * inner
-            )
-    lift = lift_ref[...]
-    jac = jac_ref[...]
-    for v in range(nvars):
-        total = dot(lift, split_rows(jump[v]))
-        for d in range(3):
-            total = total + vel[d : d + 1] * own[v][96 + 64 * d : 160 + 64 * d]
-        rate = -jac * total
-        rate_ref[v] = rate
-        hi, lo = halves(sol_ref[v] + section_step * rate)
-        hi_ref[64 * v : 64 * v + 64, :] = hi
-        lo_ref[64 * v : 64 * v + 64, :] = lo
+            total = dot(lift, split_rows(jump[v]))
+            for d in range(3):
+                total = total + vel[d : d + 1] * own[v][96 + 64 * d : 160 + 64 * d]
+            rate = -jac * total
+            rate_ref[v, :, span] = rate
+            hi, lo = halves(sol[v] + section_step * rate)
+            hi_ref[64 * v : 64 * v + 64, span] = hi
+            lo_ref[64 * v : 64 * v + 64, span] = lo
+
+    base = step * width
+    work(even, slice(0, half), odd, base + half)
+    work(odd, slice(half, 2 * half), even, jnp.minimum(base + 2 * half, last))
 
 
 def section(face_link, table, solution, velocity, inv_jacobian, face_speed, operators, lifting):
     nvars, points, elems = solution.shape
     width = 256
-    whole = lambda shape: pl.BlockSpec(shape, lambda i, links: (0,) * len(shape))
+    whole = pl.BlockSpec(memory_space=pltpu.VMEM)
     block = lambda rows: pl.BlockSpec((rows, width), lambda i, links: (0, i))
     cube = pl.BlockSpec((nvars, points, width), lambda i, links: (0, 0, i))
     pieces = jax.ShapeDtypeStruct((nvars * points, elems), jnp.bfloat16)
@@ -238,15 +265,13 @@
         grid_spec=pltpu.PrefetchScalarGridSpec(
             num_scalar_prefetch=1,
             grid=(elems // width,),
-            in_specs=[
-                whole(table.shape), cube, block(3), block(64), block(96),
-                whole(operators.shape), whole(lifting.shape),
-            ],
+            in_specs=[whole, cube, block(3), block(64), block(96), whole, whole],
             out_specs=[cube, block(nvars * points), block(nvars * points)],
             scratch_shapes=[
-                pltpu.VMEM((6, width, 128), jnp.float32),
-                pltpu.VMEM((nvars, 96, width), jnp.float32),
-                pltpu.VMEM((width // 128, 96, 128), jnp.float32),
+                pltpu.VMEM((6, 128, 128), jnp.float32),
+                pltpu.VMEM((6, 128, 128), jnp.float32),
+                pltpu.VMEM((nvars, 96, 128), jnp.float32),
+                pltpu.VMEM((96, 128), jnp.float32),
             ],
         ),
         out_shape=[jax.ShapeDtypeStruct(solution.shape, jnp.float32), pieces, pieces],
@@ -255,9 +280,16 @@
     )(face_link, table, solution, velocity, inv_jacobian, face_speed, operators, lifting)
 
 
-def receptor_kernel(buckets, nvars, hi_ref, lo_ref, donor_ref, coord_ref, owner_ref, out_ref, pieces, acc, seen, upper):
+def one_hot(rows, index, dtype=jnp.int16):
+    count = lax.broadcasted_iota(dtype, (rows, index.shape[1]), 0)
+    return jnp.where(count == index.astype(dtype), jnp.bfloat16(1), jnp.bfloat16(0))
+
+
+def receptor_kernel(buckets, nvars, hi_ref, lo_ref, donor_ref, coord_ref, owner_ref, out_ref, pieces, acc, seen):
     elems = hi_ref.shape[1]
     width = donor_ref.shape[1]
+    part = 512
+    tile = 256
     capacity = 16384 // buckets
     step = pl.program_id(0)
     rows = nvars * 64
@@ -266,41 +298,43 @@
     def _():
         pieces[:rows, :] = hi_ref[...]
         pieces[rows:, :] = lo_ref[...]
-        seen[...] = jnp.zeros_like(seen)
-        upper[...] = (
-            lax.broadcasted_iota(jnp.int32, (width, width), 0)
-            < lax.broadcasted_iota(jnp.int32, (width, width), 1)
-        ).astype(jnp.float32).astype(jnp.bfloat16)
-
-    donor = donor_ref[...]
-    chosen = (lax.broadcasted_iota(jnp.int32, (elems, width), 0) == donor)
-    chosen = chosen.astype(jnp.float32).astype(jnp.bfloat16)
-    picked = dot(pieces[...], chosen)
-    lx = lagrange_at(coord_ref[0:1, :])
-    ly = lagrange_at(coord_ref[1:2, :])
-    lz = jnp.concatenate(lagrange_at(coord_ref[2:3, :]), axis=0)
-    yz = jnp.concatenate([ly[j] * lz for j in range(4)], axis=0)
-    weights = jnp.concatenate([lx[i] * yz for i in range(4)], axis=0)
-    values = []
-    for v in range(nvars):
-        both = picked[64 * v : 64 * v + 64] + picked[rows + 64 * v : rows + 64 * v + 64]
-        values.append(jnp.sum(both * weights, axis=0, keepdims=True))
 
     owner = owner_ref[...]
     named = (lax.broadcasted_iota(jnp.int32, (16, width), 0) == owner).astype(jnp.float32)
-    before = dot(named.astype(jnp.bfloat16), upper[...]) + seen[:, 0:1]
-    rank = jnp.sum(named * before, axis=0, keepdims=True)
-    seen[...] = seen[...] + jnp.sum(named, axis=1, keepdims=True)
-    place = owner * capacity + rank.astype(jnp.int32)
-    in_row = (lax.broadcasted_iota(jnp.int32, (64, width), 0) == place // 256)
-    in_row = in_row.astype(jnp.float32).astype(jnp.bfloat16)
-    in_lane = (lax.broadcasted_iota(jnp.int32, (256, width), 0) == lax.rem(place, 256))
-    in_lane = in_lane.astype(jnp.float32).astype(jnp.bfloat16)
-    parts = []
-    for v in range(nvars):
-        for piece in halves(values[v]):
-            parts.append(in_row * piece)
-    spread = dot_nt(jnp.concatenate(parts, axis=0), in_lane)
+    upper = (
+        lax.broadcasted_iota(jnp.int32, (tile, tile), 0)
+        < lax.broadcasted_iota(jnp.int32, (tile, tile), 1)
+    ).astype(jnp.float32).astype(jnp.bfloat16)
+    tiles = [named[:, t : t + tile] for t in range(0, width, tile)]
+    before = dot(jnp.concatenate(tiles, axis=0).astype(jnp.bfloat16), upper)
+    carry = jnp.where(step == 0, 0.0, seen[...])[:, 0:1]
+    ranks = []
+    for t, own in enumerate(tiles):
+        ranks.append(jnp.sum(own * (before[16 * t : 16 * t + 16] + carry), axis=0, keepdims=True))
+        carry = carry + jnp.sum(own, axis=1, keepdims=True)
+    seen[...] = jnp.broadcast_to(carry, seen.shape)
+    place = owner * capacity + jnp.concatenate(ranks, axis=1).astype(jnp.int32)
+    in_row = one_hot(64, place // 256)
+    in_lane = one_hot(256, lax.rem(place, 256))
+
+    both_pieces = pieces[...]
+    columns = []
+    for start in range(0, width, part):
+        span = slice(start, start + part)
+        picked = dot(both_pieces, one_hot(elems, donor_ref[:, span]))
+        lx = lagrange_at(coord_ref[0:1, span])
+        ly = lagrange_at(coord_ref[1:2, span])
+        lz = jnp.concatenate(lagrange_at(coord_ref[2:3, span]), axis=0)
+        yz = jnp.concatenate([ly[j] * lz for j in range(4)], axis=0)
+        weights = jnp.concatenate([lx[i] * yz for i in range(4)], axis=0)
+        parts = []
+        for v in range(nvars):
+            both = picked[64 * v : 64 * v + 64] + picked[rows + 64 * v : rows + 64 * v + 64]
+            value = jnp.sum(both * weights, axis=0, keepdims=True)
+            for piece in halves(value):
+                parts.append(in_row[:, span] * piece)
+        columns.append(jnp.concatenate(parts, axis=0))
+    spread = dot_nt(jnp.concatenate(columns, axis=1), in_lane)
     acc[...] = jnp.where(step == 0, 0.0, acc[...]) + spread
 
     @pl.when(step == pl.num_programs(0) - 1)
@@ -315,8 +349,8 @@
     rows, elems = hi.shape
     nvars = rows // 64
     receptors = donors.shape[1]
-    width = 512
-    whole = pl.BlockSpec((rows, elems), lambda i: (0, 0))
+    width = 2048
+    whole = pl.BlockSpec(memory_space=pltpu.VMEM)
     block = lambda count: pl.BlockSpec((count, width), lambda i: (0, i))
     return pl.pallas_call(
         functools.partial(receptor_kernel, buckets, nvars),
@@ -328,7 +362,6 @@
             pltpu.VMEM((2 * rows, elems), jnp.bfloat16),
             pltpu.VMEM((128 * nvars, 256), jnp.float32),
             pltpu.VMEM((16, 128), jnp.float32),
-            pltpu.VMEM((width, width), jnp.bfloat16),
         ],
         compiler_params=pltpu.CompilerParams(vmem_limit_bytes=VMEM_BYTES),
         name="receptor_slots",

time: 67.9 us -> 60 us (0.88)
  local copies, waits for them, and re-layouts: 6.36 us -> 1.87 us
  Pallas kernels: 60.3 us -> 56.7 us
    pallas_call x1, Pallas kernels: 26.4 us -> 16.9 us  [receptor_slots(): pl.pallas_call(functools.partial(receptor_kernel, buckets, nvars), grid=(...]
    unnamed x25 -> x1, local copies, waits for them, and re-layouts: 6.36 us -> 1.87 us
    pallas_call x1, Pallas kernels: 5.63 us -> 9.89 us  [face_table(): pl.pallas_call(table_kernel, out_shape=jax.ShapeDtypeStruct((6 * elems +...]
    pallas_call x1, Pallas kernels: 11.1 us -> 12.7 us  [exchange(): pl.pallas_call(functools.partial(exchange_kernel, buckets, nvars), out_sh...]
where the time goes in v2:
time: 60 us; the launch traced here: 59.2 us
  Pallas kernels  56.7 us (94%)
  local copies, waits for them, and re-layouts  1.87 us (3%)
  between operations  0.65 us (1%)
    pallas_call x1, Pallas kernels, section(): pl.pallas_call(section_kernel, grid_spec=pltpu.PrefetchScalarGridSpec(num...  17.2 us
    pallas_call x1, Pallas kernels, receptor_slots(): pl.pallas_call(functools.partial(receptor_kernel, buckets, nvars), grid=(...  16.9 us
    pallas_call x1, Pallas kernels, exchange(): pl.pallas_call(functools.partial(exchange_kernel, buckets, nvars), out_sh...  12.7 us
    pallas_call x1, Pallas kernels, face_table(): pl.pallas_call(table_kernel, out_shape=jax.ShapeDtypeStruct((6 * elems +...  9.89 us
    unnamed x1, local copies, waits for them, and re-layouts  1.87 us

profile of v2, /device:TPU:0, one launch (start us, length us, event | category | flops | bytes accessed | tf_op | source)
XLA Modules:
  0.0 59.2 jit_solution(2591261275702799081)
XLA Ops:
  0.6 9.9 %face_table.1.table_ref = f32[6272,128]{1,0:T(8,128)} custom-call(f32[5,64,1024]{2,1,0:T(8,128)} %sol_ref.1, f32[96,1024]{1,0:T(8,128)} %speed_ref.1, s32[6,1024]{1,0:T(8,128)} %links_ref.1, bf16[96,192]{1,0:T(8,128)(2,1)} %constant.6.clone.ext_ref), custom_call_target="tpu_custom_call" | custom-call | tf_op jit(solution)/shard_map/face_table/pallas_call | solution.py:174
  10.5 17.2 %section.1 = (f32[5,64,1024]{2,1,0:T(8,128)}, bf16[320,1024]{1,0:T(8,128)(2,1)}, bf16[320,1024]{1,0:T(8,128)(2,1)}) custom-call(s32[6,1024]{1,0:T(8,128)} %links_ref.1, f32[6272,128]{1,0:T(8,128)} %face_table.1.table_ref, f32[5,64,1024]{2,1,0:T(8,128)} %sol_ref.1, f32[3,1024]{1,0:T(4,128)} %vel_ref.1, f32[64,1024]{1,0:T(8,128)} %jac_ref.1, ...), custom_call_target="tpu_custom_call" | custom-call | tf_op jit(solution)/shard_map/section/pallas_call | solution.py:263
  27.7 16.9 %receptor_slots.1.send_ref = f32[640,128]{1,0:T(8,128)} custom-call(bf16[320,1024]{1,0:T(8,128)(2,1)} %get-tuple-element.6.hi_ref, bf16[320,1024]{1,0:T(8,128)(2,1)} %get-tuple-element.7.lo_ref, s32[1,8192]{1,0:T(1,128)} %bitcast.2, f32[3,8192]{1,0:T(4,128)} %coord_ref.1, s32[1,8192]{1,0:T(1,128)} %bitcast.3), custom_call_target="tpu_custom_call" | custom-call | tf_op jit(solution)/shard_map/receptor_slots/pallas_call | solution.py:355
  44.6 12.7 %exchange.1 = f32[5,16384]{1,0:T(8,128)} custom-call(f32[640,128]{1,0:T(8,128)} %receptor_slots.1.send_ref), custom_call_target="tpu_custom_call" | custom-call | tf_op jit(solution)/shard_map/exchange/pallas_call | solution.py:401
  57.3 1.9 %copy.14 = f32[5,16384]{1,0:T(8,128)} copy(f32[5,16384]{1,0:T(8,128)} %exchange.1) | data formatting | bytes 655360

commit v3 on v2

--- a/solution.py
+++ b/solution.py
@@ -12,7 +12,7 @@
 quad_weights = (0.3478548451374538, 0.6521451548625461, 0.6521451548625461, 0.3478548451374538)
 section_step = 0.2
 MESH = pl.DeviceIdType.MESH
-VMEM_BYTES = 56 * 1024 * 1024
+VMEM_BYTES = 32 * 1024 * 1024
 
 
 def lagrange_at(x):
@@ -105,16 +105,9 @@
 
 
 def table_kernel(
-    sol_hbm, speed_hbm, links_hbm, ext_ref, table_ref,
-    sol_ref, speed_ref, links_ref, nat, tiles, out_rows, in_rows, fetch_sem, send_sem, recv_sem,
+    sol_ref, speed_ref, links_ref, ext_ref, table_ref, nat, tiles, out_rows, in_rows, send_sem, recv_sem
 ):
     nvars, _, elems = sol_ref.shape
-    fetches = [pltpu.make_async_copy(speed_hbm, speed_ref, fetch_sem.at[nvars])]
-    for v in range(nvars):
-        fetches.append(pltpu.make_async_copy(sol_hbm.at[v], sol_ref.at[v], fetch_sem.at[v]))
-    fetches.append(pltpu.make_async_copy(links_hbm, links_ref, fetch_sem.at[nvars + 1]))
-    for fetch in fetches:
-        fetch.start()
     faces_total = 6 * elems
     rim = in_rows.shape[0] // 2
     size = lax.axis_size("valve")
@@ -124,14 +117,11 @@
     for peer in (up, down):
         pl.semaphore_signal(barrier, inc=1, device_id={"valve": peer}, device_id_type=MESH)
     ext = ext_ref[...]
-    fetches[0].wait()
     speeds = by_face(speed_ref, tiles)
     for v in range(nvars):
-        fetches[v + 1].wait()
         vals = dot(ext, split_rows(sol_ref[v]))
         for f in range(6):
             nat[f, 16 * v : 16 * v + 16, :] = vals[16 * f : 16 * f + 16]
-    fetches[nvars + 1].wait()
     picked = jnp.zeros((2 * rim, 128), jnp.float32)
     slot = lax.broadcasted_iota(jnp.int32, (2 * rim, elems), 0) + faces_total
     for f in range(6):
@@ -174,17 +164,13 @@
     return pl.pallas_call(
         table_kernel,
         out_shape=jax.ShapeDtypeStruct((6 * elems + 2 * rim, 128), jnp.float32),
-        in_specs=[pl.BlockSpec(memory_space=pl.ANY)] * 3 + [vmem],
+        in_specs=[vmem] * 4,
         out_specs=vmem,
         scratch_shapes=[
-            pltpu.VMEM(solution.shape, jnp.float32),
-            pltpu.VMEM(face_speed.shape, jnp.float32),
-            pltpu.VMEM(face_link.shape, jnp.int32),
             pltpu.VMEM((6, 128, elems), jnp.float32),
             pltpu.VMEM((elems // 128, 96, 128), jnp.float32),
             pltpu.VMEM((2 * rim, 128), jnp.float32),
             pltpu.VMEM((2 * rim, 128), jnp.float32),
-            pltpu.SemaphoreType.DMA((solution.shape[0] + 2,)),
             pltpu.SemaphoreType.DMA((2,)),
             pltpu.SemaphoreType.DMA((2,)),
         ],
@@ -207,7 +193,7 @@
     lift = lift_ref[...]
 
     def fetch(rows, f, u, start):
-        rows[f, pl.ds(u, 1), :] = table_ref[pl.ds(links_ref[f, start + u], 1), :]
+        rows[f, pl.ds(u, 1), :] = table_ref[links_ref[f, start + u]]
 
     @pl.when(step == 0)
     def _():
@@ -277,7 +263,7 @@
         out_shape=[jax.ShapeDtypeStruct(solution.shape, jnp.float32), pieces, pieces],
         compiler_params=pltpu.CompilerParams(vmem_limit_bytes=VMEM_BYTES),
         name="section",
-    )(face_link, table, solution, velocity, inv_jacobian, face_speed, operators, lifting)
+    )(face_link, table.reshape(-1, 1, 128), solution, velocity, inv_jacobian, face_speed, operators, lifting)
 
 
 def one_hot(rows, index, dtype=jnp.int16):

time: 60 us -> 52.8 us (0.88)
  Pallas kernels: 56.7 us -> 46.9 us
  local copies, waits for them, and re-layouts: 1.87 us -> 4.69 us
    pallas_call x1, Pallas kernels: 9.89 us -> 5.63 us  [face_table(): pl.pallas_call(table_kernel, out_shape=jax.ShapeDtypeStruct((6 * elems +...]
    unnamed x1 -> x23, local copies, waits for them, and re-layouts: 1.87 us -> 4.69 us
    pallas_call x1, Pallas kernels: 16.9 us -> 14.8 us  [receptor_slots(): pl.pallas_call(functools.partial(receptor_kernel, buckets, nvars), grid=(...]
    pallas_call x1, Pallas kernels: 17.2 us -> 15.4 us  [section(): pl.pallas_call(section_kernel, grid_spec=pltpu.PrefetchScalarGridSpec(num...]
    pallas_call x1, Pallas kernels: 12.7 us -> 11.1 us  [exchange(): pl.pallas_call(functools.partial(exchange_kernel, buckets, nvars), out_sh...]
where the time goes in v3:
time: 52.8 us; the launch traced here: 52.3 us
  Pallas kernels  46.9 us (89%)
  local copies, waits for them, and re-layouts  4.69 us (9%)
  between operations  0.73 us (1%)
    pallas_call x1, Pallas kernels, section(): pl.pallas_call(section_kernel, grid_spec=pltpu.PrefetchScalarGridSpec(num...  15.4 us
    pallas_call x1, Pallas kernels, receptor_slots(): pl.pallas_call(functools.partial(receptor_kernel, buckets, nvars), grid=(...  14.8 us
    pallas_call x1, Pallas kernels, exchange(): pl.pallas_call(functools.partial(exchange_kernel, buckets, nvars), out_sh...  11.1 us
    pallas_call x1, Pallas kernels, face_table(): pl.pallas_call(table_kernel, out_shape=jax.ShapeDtypeStruct((6 * elems +...  5.63 us
    unnamed x23, local copies, waits for them, and re-layouts  4.69 us

profile of v3, /device:TPU:0, one launch (start us, length us, event | category | flops | bytes accessed | tf_op | source)
XLA Modules:
  0.0 52.3 jit_solution(8567601884269466937)
XLA Ops:
  0.6 0.0 copy-start
  0.6 1.3 %copy-done = f32[5,64,1024]{2,1,0:T(8,128)S(1)} copy-done((f32[5,64,1024]{2,1,0:T(8,128)S(1)}, f32[5,64,1024]{2,1,0:T(8,128)}, u32[]{:S(2)}) %copy-start) | copy-done | bytes 1310744
  1.9 0.0 copy-start.1
  2.0 1.0 %copy-done.1 = f32[96,1024]{1,0:T(8,128)S(1)} copy-done((f32[96,1024]{1,0:T(8,128)S(1)}, f32[96,1024]{1,0:T(8,128)}, u32[]{:S(2)}) %copy-start.1) | copy-done | bytes 393240
  2.9 0.0 copy-start.4
  2.9 0.8 %copy-done.4 = s32[6,1024]{1,0:T(8,128)S(1)} copy-done((s32[6,1024]{1,0:T(8,128)S(1)}, s32[6,1024]{1,0:T(8,128)}, u32[]{:S(2)}) %copy-start.4) | copy-done | bytes 24600
  3.7 0.0 copy-start.6
  3.7 0.8 %copy-done.6 = bf16[96,192]{1,0:T(8,128)(2,1)S(1)} copy-done((bf16[96,192]{1,0:T(8,128)(2,1)S(1)}, bf16[96,192]{1,0:T(8,128)(2,1)}, u32[]{:S(2)}) %copy-start.6) | copy-done | bytes 36888
  4.5 0.0 copy-start.2
  4.5 0.0 copy-start.3
  4.5 0.0 copy-start.7
  4.5 0.0 copy-start.10
  4.5 5.6 %face_table.1 = f32[6272,128]{1,0:T(8,128)S(1)} custom-call(f32[5,64,1024]{2,1,0:T(8,128)S(1)} %copy-done, f32[96,1024]{1,0:T(8,128)S(1)} %copy-done.1, s32[6,1024]{1,0:T(8,128)S(1)} %copy-done.4, bf16[96,192]{1,0:T(8,128)(2,1)S(1)} %copy-done.6), custom_call_target="tpu_custom_call" | custom-call | tf_op jit(solution)/shard_map/face_table/pallas_call | solution.py:164
  10.2 0.0 copy-done.2
  10.2 0.0 copy-done.3
  10.2 0.0 copy-done.7
  10.2 0.0 copy-done.10
  10.2 0.0 copy-start.5
  10.2 0.0 copy-start.8
  10.2 0.0 copy-start.9
  10.2 15.4 %section.1 = (f32[5,64,1024]{2,1,0:T(8,128)}, bf16[320,1024]{1,0:T(8,128)(2,1)S(1)}, bf16[320,1024]{1,0:T(8,128)(2,1)S(1)}) custom-call(s32[6,1024]{1,0:T(8,128)S(1)} %copy-done.4, f32[6272,1,128]{2,1,0:T(1,128)S(1)} %bitcast.3, f32[5,64,1024]{2,1,0:T(8,128)S(1)} %copy-done, f32[3,1024]{1,0:T(4,128)S(1)} %copy-done.10, f32[64,1024]{1,0:T(8,128)S(1)} %copy-done.2, ...), custom_call_target="tpu_custom_call" | custom-call | tf_op jit(solution)/shard_map/section/pallas_call | solution.py:249
  25.6 0.0 copy-done.5
  25.6 0.0 copy-done.8
  25.6 0.0 copy-done.9
  25.6 14.8 %receptor_slots.1.send_ref = f32[640,128]{1,0:T(8,128)S(1)} custom-call(bf16[320,1024]{1,0:T(8,128)(2,1)S(1)} %get-tuple-element.6.hi_ref, bf16[320,1024]{1,0:T(8,128)(2,1)S(1)} %get-tuple-element.7.lo_ref, s32[1,8192]{1,0:T(1,128)S(1)} %bitcast.4, f32[3,8192]{1,0:T(4,128)S(1)} %copy-done.5, s32[1,8192]{1,0:T(1,128)S(1)} %bitcast.5), custom_call_target="tpu_custom_call" | custom-call | tf_op jit(solution)/shard_map/receptor_slots/pallas_call | solution.py:341
  40.4 11.1 %exchange.1 = f32[5,16384]{1,0:T(8,128)S(1)} custom-call(f32[640,128]{1,0:T(8,128)S(1)} %receptor_slots.1.send_ref), custom_call_target="tpu_custom_call" | custom-call | tf_op jit(solution)/shard_map/exchange/pallas_call | solution.py:387
  51.5 0.8 %copy.14 = f32[5,16384]{1,0:T(8,128)} copy(f32[5,16384]{1,0:T(8,128)S(1)} %exchange.1) | data formatting | bytes 655360
Async XLA Ops:
  0.6 1.3 %copy-start = (f32[5,64,1024]{2,1,0:T(8,128)S(1)}, f32[5,64,1024]{2,1,0:T(8,128)}, u32[]{:S(2)}) copy-start(f32[5,64,1024]{2,1,0:T(8,128)} %sol_ref.3) | copy-start | bytes 3932164
  1.9 1.0 %copy-start.1 = (f32[96,1024]{1,0:T(8,128)S(1)}, f32[96,1024]{1,0:T(8,128)}, u32[]{:S(2)}) copy-start(f32[96,1024]{1,0:T(8,128)} %speed_ref.3) | copy-start | bytes 1179652
  2.9 0.8 %copy-start.4 = (s32[6,1024]{1,0:T(8,128)S(1)}, s32[6,1024]{1,0:T(8,128)}, u32[]{:S(2)}) copy-start(s32[6,1024]{1,0:T(8,128)} %links_ref.3) | copy-start | bytes 73732
  3.7 0.8 %copy-start.6 = (bf16[96,192]{1,0:T(8,128)(2,1)S(1)}, bf16[96,192]{1,0:T(8,128)(2,1)}, u32[]{:S(2)}) copy-start(bf16[96,192]{1,0:T(8,128)(2,1)} %constant.6.clone.ext_ref) | copy-start | bytes 110596
  4.5 5.7 %copy-start.2 = (f32[64,1024]{1,0:T(8,128)S(1)}, f32[64,1024]{1,0:T(8,128)}, u32[]{:S(2)}) copy-start(f32[64,1024]{1,0:T(8,128)} %jac_ref.1) | copy-start | bytes 786436
  4.5 5.7 %copy-start.3 = (bf16[288,192]{1,0:T(8,128)(2,1)S(1)}, bf16[288,192]{1,0:T(8,128)(2,1)}, u32[]{:S(2)}) copy-start(bf16[288,192]{1,0:T(8,128)(2,1)} %constant.7.clone.ops_ref) | copy-start | bytes 331780
  4.5 5.7 %copy-start.7 = (bf16[64,288]{1,0:T(8,128)(2,1)S(1)}, bf16[64,288]{1,0:T(8,128)(2,1)}, u32[]{:S(2)}) copy-start(bf16[64,288]{1,0:T(8,128)(2,1)} %constant.8.clone.lift_ref) | copy-start | bytes 110596
  4.5 5.7 %copy-start.10 = (f32[3,1024]{1,0:T(4,128)S(1)}, f32[3,1024]{1,0:T(4,128)}, u32[]{:S(2)}) copy-start(f32[3,1024]{1,0:T(4,128)} %vel_ref.1) | copy-start | bytes 36868
  10.2 15.4 %copy-start.5 = (f32[3,8192]{1,0:T(4,128)S(1)}, f32[3,8192]{1,0:T(4,128)}, u32[]{:S(2)}) copy-start(f32[3,8192]{1,0:T(4,128)} %coord_ref.1) | copy-start | bytes 294916
  10.2 15.4 %copy-start.8 = (s32[8192]{0:T(1024)S(1)}, s32[8192]{0:T(1024)}, u32[]{:S(2)}) copy-start(s32[8192]{0:T(1024)} %param.16) | copy-start | bytes 98308
  10.2 15.4 %copy-start.9 = (s32[8192,1]{0,1:T(1,128)S(1)}, s32[8192,1]{0,1:T(1,128)}, u32[]{:S(2)}) copy-start(s32[8192,1]{0,1:T(1,128)} %param.18) | copy-start | bytes 98308
